TPU v7x, 128 devices: a whole 4x4x4 slice. The times are simulated.
128 devices in a mesh: seq: 32 (over x, y, core), batch: 4 (over z).
Axes of the slice: x: 4, y: 4, z: 4, core: 2. Of those that a mesh axis runs over, the one named last changes fastest.
Arguments:
- tokens: bfloat16 [4, 16384, 2048], P('batch', 'seq'), may hold values from -6 to 6
- w_qkv: bfloat16 [2048, 3072], replicated, may hold values from -0.125 to 0.125
- cotangent: bfloat16 [4, 16384, 1024], P('batch', 'seq'), may hold values from -6 to 6
Outputs:
- attended: bfloat16 [4, 16384, 1024], P('batch', 'seq')
- token_grad: bfloat16 [4, 16384, 2048], P('batch', 'seq')
- weight_grad: float32 [2048, 3072], P('seq')
All inputs are finite; a program needn't handle non-finite values.
Results may differ from a plain program's by a relative error of at most 0.0064.
Values sent between devices are 32-bit elements; how exact they have to be, the bound alone decides.
No kernel may reach another device: no remote copies, remote signals or barrier semaphores. Data moves between devices by JAX's collectives and lax.ppermute only.
A program may use at most 192 MiB of HBM per device.

v0:
```python
import jax
import jax.numpy as jnp
from jax import lax
from jax.sharding import PartitionSpec as P

HEADS = 8
DH = 128
BLK = 512


PRECISE = lax.Precision.HIGHEST


def entering(value, axis, combine, identity, reverse):
    devices, position = (lax.axis_size(axis), lax.axis_index(axis))
    everything = lax.all_gather(value, axis)
    start = jnp.broadcast_to(jnp.asarray(identity, value.dtype), value.shape)

    def step(k, before):
        at = devices - 1 - k if reverse else k
        reached = at > position if reverse else at < position
        new = combine(before, everything[at])
        return jnp.where(reached, new, before)

    return lax.fori_loop(0, devices, step, start)


def add_states(earlier, latter):
    return earlier + latter


def running_states(block_states, incoming, reverse):
    zero_block = jnp.zeros_like(block_states)
    if reverse:
        totals = jnp.cumsum(block_states[::-1], axis=0)[::-1]
        return incoming[None] + jnp.concatenate([totals[1:], zero_block], 0)
    totals = jnp.cumsum(block_states, axis=0)
    return incoming[None] + jnp.concatenate([zero_block, totals[:-1]], 0)


def body(tokens, w_qkv, cotangent):
    row_count = tokens.shape[1]
    width = w_qkv.shape[1] // 3
    block_count = row_count // BLK
    seq_count = lax.axis_size("seq")
    batch_count = lax.axis_size("batch")
    local_x = tokens[0]
    projected = jnp.dot(local_x, w_qkv, preferred_element_type=jnp.float32).astype(jnp.bfloat16)
    queries = projected[:, :width].reshape(block_count, BLK, HEADS, DH)
    key_heads = projected[:, width : 2 * width].reshape(block_count, BLK, HEADS, DH)
    value_heads = projected[:, 2 * width :].reshape(block_count, BLK, HEADS, DH)
    position = lax.axis_index("seq") * row_count + jnp.arange(row_count, dtype=jnp.int32)
    pos_scale = DH ** (-0.5) / jnp.sqrt(position.astype(jnp.float32) + 1.0)
    scaled_grad = (cotangent[0].astype(jnp.float32) * pos_scale[:, None]).astype(jnp.bfloat16)
    grad_heads = scaled_grad.reshape(block_count, BLK, HEADS, DH)
    kv_blocks = jnp.einsum(
        "nrha,nrhb->nhab", key_heads, value_heads, preferred_element_type=jnp.float32
    )
    grad_blocks = jnp.einsum(
        "nrha,nrhb->nhab", queries, grad_heads, preferred_element_type=jnp.float32
    )
    kv_local = jnp.sum(kv_blocks, 0)
    grad_local = jnp.sum(grad_blocks, 0)
    zero_state = jnp.zeros_like(kv_local)
    kv_in = entering(kv_local, "seq", add_states, zero_state, False)
    grad_in = entering(grad_local, "seq", add_states, zero_state, True)
    kv_before = running_states(kv_blocks, kv_in, False)
    grad_after = running_states(grad_blocks, grad_in, True)
    causal = jnp.arange(BLK)[:, None] >= jnp.arange(BLK)[None, :]
    scores = jnp.where(
        causal,
        jnp.einsum("nihd,njhd->nhij", queries, key_heads, preferred_element_type=jnp.float32),
        0.0,
    ).astype(jnp.bfloat16)
    grad_scores = jnp.where(
        causal,
        jnp.einsum("nihd,njhd->nhij", grad_heads, value_heads, preferred_element_type=jnp.float32),
        0.0,
    ).astype(jnp.bfloat16)
    query_wide = queries.astype(jnp.float32)
    key_wide = key_heads.astype(jnp.float32)
    value_wide = value_heads.astype(jnp.float32)
    grad_wide = grad_heads.astype(jnp.float32)
    attended = jnp.einsum(
        "nhij,njhd->nihd", scores, value_heads, preferred_element_type=jnp.float32
    )
    attended = attended + jnp.einsum("nihd,nhde->nihe", query_wide, kv_before, precision=PRECISE)
    attended = attended * pos_scale.reshape(block_count, BLK, 1, 1)
    query_grad = jnp.einsum(
        "nhij,njhd->nihd", grad_scores, key_heads, preferred_element_type=jnp.float32
    )
    query_grad = query_grad + jnp.einsum("nihe,nhde->nihd", grad_wide, kv_before, precision=PRECISE)
    key_grad = jnp.einsum(
        "nhij,nihd->njhd", grad_scores, queries, preferred_element_type=jnp.float32
    )
    key_grad = key_grad + jnp.einsum("njhe,nhde->njhd", value_wide, grad_after, precision=PRECISE)
    value_grad = jnp.einsum(
        "nhij,nihe->njhe", scores, grad_heads, preferred_element_type=jnp.float32
    )
    value_grad = value_grad + jnp.einsum("njhd,nhde->njhe", key_wide, grad_after, precision=PRECISE)
    qkv_grad = jnp.concatenate(
        [
            query_grad.reshape(row_count, width),
            key_grad.reshape(row_count, width),
            value_grad.reshape(row_count, width),
        ],
        1,
    ).astype(jnp.bfloat16)
    token_grad = lax.dot_general(
        qkv_grad, w_qkv, (((1,), (1,)), ((), ())), preferred_element_type=jnp.float32
    )
    token_grad = token_grad.astype(jnp.bfloat16)[None]
    partial_rows = lax.psum_scatter(
        lax.dot_general(
            local_x, qkv_grad, (((0,), (0,)), ((), ())), preferred_element_type=jnp.float32
        ),
        "seq",
        scatter_dimension=0,
        tiled=True,
    )
    summed = lax.psum(partial_rows, "batch")
    grad_scale = 1.0 / jnp.sqrt(jnp.float32(batch_count * seq_count * row_count))
    weight_grad = summed * grad_scale
    return (attended.reshape(row_count, width).astype(jnp.bfloat16)[None], token_grad, weight_grad)


def solution(mesh):
    return jax.shard_map(
        body,
        mesh=mesh,
        in_specs=(P("batch", "seq", None), P(), P("batch", "seq", None)),
        out_specs=(P("batch", "seq", None), P("batch", "seq", None), P("seq", None)),
        check_vma=False,
    )
```

profile of v0, /device:TPU:1, one launch (start us, length us, event | category | flops | bytes accessed | tf_op | source)
XLA Modules:
  0.0 470.0 jit_solution(5474588875437159934)
XLA Ops:
  7.2 1.5 copy-done
  8.8 9.6 %convolution_convert_fusion = bf16[512,3072]{1,0:T(8,128)(2,1)S(1)} fusion(bf16[2048,3072]{1,0:T(8,128)(2,1)} %param.8, bf16[1,512,2048]{2,1,0:T(8,128)(2,1)S(1)} %copy-done), kind=kOutput, calls=%fused_computation.5 | convolution fusion | flops 6444023808 | bytes 17825792 | tf_op jit(solution)/shard_map/dot_general | solution.py:48
  18.4 2.2 slice_bitcast_fusion.2
  21.9 2.5 copy.29
  24.3 2.8 fusion.10
  27.2 2.6 copy.51
  29.8 2.3 copy.54
  32.0 2.0 multiply_convert_fusion
  36.4 3.1 select_convert_fusion
  39.5 1.5 select_convert_fusion.1
  41.0 2.1 fusion.21
  43.1 2.8 fusion.20
  45.9 2.1 fusion.23
  47.9 55.3 %all-gather.5.cloned.1.call-done = f32[256,128,128]{2,1,0:T(8,128)} async-done(((f32[8,128,128]{2,1,0:T(8,128)}), f32[256,128,128]{2,1,0:T(8,128)}) %all-gather.5.cloned.1.call-update) | async-done | bytes 16777232 | tf_op jit(solution)/shard_map/all_gather | solution.py:16
  103.3 40.3 %while.30 = (s32[]{:T(128)}, f32[8,128,128]{2,1,0:T(8,128)S(1)}, s32[]{:T(128)}, f32[32,8,128,128]{3,2,1,0:T(8,128)}, s32[]{:T(128)}, /*index=5*/s32[]{:T(128)}) while((s32[]{:T(128)}, f32[8,128,128]{2,1,0:T(8,128)S(1)}, s32[]{:T(128)}, f32[32,8,128,128]{3,2,1,0:T(8,128)}, s32[]{:T(128)}, /*index=5*/s32[]{:T(128)}) %tuple.91), condition=%wide.region_1.0_spmd.clone, body=%wide.region_0.0_spmd.clone.sunk | while | flops 393220 | bytes 1572965 | solution.py:25
  113.3 1.3 add_select_fusion.4
  114.6 1.3 add_select_fusion.4
  138.4 1.4 add_select_fusion.4
  143.6 33.9 %all-gather.7.cloned.1.call-done = f32[256,128,128]{2,1,0:T(8,128)} async-done(((f32[8,128,128]{2,1,0:T(8,128)}), f32[256,128,128]{2,1,0:T(8,128)}) %all-gather.7.cloned.1.call-update) | async-done | bytes 16777232 | tf_op jit(solution)/shard_map/all_gather | solution.py:16
  177.4 40.2 %while.31 = (s32[]{:T(128)}, f32[8,128,128]{2,1,0:T(8,128)S(1)}, s32[]{:T(128)}, f32[32,8,128,128]{3,2,1,0:T(8,128)}, s32[]{:T(128)}, /*index=5*/s32[]{:T(128)}, s32[]{:T(128)}, s32[]{:T(128)}) while((s32[]{:T(128)}, f32[8,128,128]{2,1,0:T(8,128)S(1)}, s32[]{:T(128)}, f32[32,8,128,128]{3,2,1,0:T(8,128)}, s32[]{:T(128)}, ...), condition=%wide.region_3.4_spmd.clone, body=%wide.region_2.3_spmd.clone.sunk | while | flops 393224 | bytes 1573027 | solution.py:25
  217.6 3.1 add_convert_fusion
  225.6 15.1 %convolution_bitcast_fusion = f32[2048,3072]{0,1:T(8,128)} fusion(bf16[1,512,2048]{2,1,0:T(8,128)(2,1)S(1)} %copy-done, bf16[512,1024]{0,1:T(8,128)(2,1)S(1)} %bitcast.92, bf16[512,1024]{0,1:T(8,128)(2,1)S(1)} %bitcast.94, bf16[512,1024]{0,1:T(8,128)(2,1)S(1)} %bitcast.96), kind=kOutput, calls=%fused_computation.2 | convolution fusion | flops 6451888128 | bytes 30408704 | tf_op jit(solution)/shard_map/dot_general | solution.py:114
  240.7 24.8 %copy.52 = f32[2048,3072]{1,0:T(8,128)} copy(f32[2048,3072]{0,1:T(8,128)} %convolution_bitcast_fusion) | data formatting | bytes 50331648
  266.7 5.1 %fusion.6 = f32[8,128,512]{2,1,0:T(8,128)} fusion(bf16[8,512,512]{2,1,0:T(8,128)(2,1)} %copy-done.2, bf16[64,8,8,128]{3,2,1,0:T(8,128)(2,1)S(1)} %copy-done.4), kind=kOutput, calls=%fused_computation.19 | convolution fusion | flops 536870912 | bytes 7340032 | tf_op jit(solution)/shard_map/nhij,njhd->nihd/dot_general | solution.py:84
  271.8 133.5 %reduce-scatter.4.cloned.1.call-done = f32[64,3072]{1,0:T(8,128)} async-done(((f32[2048,3072]{1,0:T(8,128)}), f32[64,3072]{1,0:T(8,128)}) %reduce-scatter.4.cloned.1.call-update) | async-done | bytes 786448
  405.3 2.7 copy.53
  408.1 11.7 %fusion = bf16[1,512,2048]{2,1,0:T(8,128)(2,1)} fusion(bf16[2048,3072]{1,0:T(8,128)(2,1)} %param.8, bf16[512,1024]{0,1:T(8,128)(2,1)S(1)} %bitcast.93, bf16[512,1024]{0,1:T(8,128)(2,1)} %bitcast.95, bf16[512,1024]{0,1:T(8,128)(2,1)} %bitcast.97), kind=kOutput, calls=%fused_computation.8 | convolution fusion | flops 6452936704 | bytes 17825792 | tf_op jit(solution)/shard_map/dot_general | solution.py:109
  419.7 2.1 fusion.1
  421.9 2.4 copy.44
  424.3 33.8 %all-reduce.2.cloned.1.call-done = f32[64,3072]{0,1:T(8,128)} async-done(((f32[64,3072]{0,1:T(8,128)}), f32[64,3072]{0,1:T(8,128)}) %all-reduce.2.cloned.1.call-update) | async-done | bytes 786448 | tf_op jit(solution)/shard_map/psum | solution.py:121
  458.0 2.7 broadcast_multiply_fusion
  460.7 2.7 copy.45
  (116 shorter events, 84.6 us)
Async XLA Ops:
  7.2 1.6 copy-start
  7.2 96.1 %all-gather.5.cloned.1.call-start = ((), (), s32[]{:S(2)}) async-start(), calls=%async_computation.2 | async-start | bytes 17301504 | tf_op jit(solution)/shard_map/all_gather | solution.py:16
  27.1 150.3 %all-gather.7.cloned.1.call-start = ((), (), s32[]{:S(2)}) async-start(), calls=%async_computation.3 | async-start | bytes 17301504 | tf_op jit(solution)/shard_map/all_gather | solution.py:16
  32.0 3.0 copy-start.5
  34.0 1.0 copy-start.8
  36.2 369.0 %reduce-scatter.4.cloned.1.call-start = ((), (), s32[]{:S(2)}) async-start(), calls=%async_computation.4 | async-start | bytes 25952256
  36.4 3.1 copy-start.6
  36.4 3.1 copy-start.15
  41.0 4.9 %copy-start.2 = (bf16[8,512,512]{2,1,0:T(8,128)(2,1)}, bf16[8,512,512]{2,1,0:T(8,128)(2,1)S(1)}, u32[]{:S(2)}) copy-start(bf16[8,512,512]{2,1,0:T(8,128)(2,1)S(1)} %select_convert_fusion.1) | copy-start | bytes 12582916
  41.0 2.1 copy-start.11
  43.1 2.8 copy-start.9
  217.6 3.1 copy-start.3
  217.6 3.1 copy-start.13
  220.8 3.8 copy-start.16
  220.8 1.6 copy-start.10
  220.8 2.7 copy-start.12
  221.9 2.6 copy-start.18
  224.5 1.1 copy-start.19
  265.5 1.2 copy-start.4
  265.5 192.5 %all-reduce.2.cloned.1.call-start = ((), (), s32[]{:S(2)}) async-start(), calls=%async_computation.1 | async-start | bytes 3145728 | tf_op jit(solution)/shard_map/psum | solution.py:121
  271.8 136.3 %copy-start.17 = (bf16[8,128,512]{2,1,0:T(8,128)(2,1)S(1)}, bf16[8,128,512]{2,1,0:T(8,128)(2,1)}, u32[]{:S(2)}) copy-start(bf16[8,128,512]{2,1,0:T(8,128)(2,1)} %copy-done.16) | copy-start | bytes 3145732
  408.0 11.7 %copy-start.7 = (bf16[512,1024]{0,1:T(8,128)(2,1)S(1)}, bf16[512,1024]{0,1:T(8,128)(2,1)}, u32[]{:S(2)}) copy-start(bf16[512,1024]{0,1:T(8,128)(2,1)} %copy.54) | copy-start | bytes 3145732
  408.1 11.7 %copy-start.14 = (f32[8,128,512]{2,1,0:T(8,128)S(1)}, f32[8,128,512]{2,1,0:T(8,128)}, u32[]{:S(2)}) copy-start(f32[8,128,512]{2,1,0:T(8,128)} %fusion.6) | copy-start | bytes 6291460
  421.9 41.6 %copy-start.1 = (bf16[1,512,2048]{2,1,0:T(8,128)(2,1)S(1)}, bf16[1,512,2048]{2,1,0:T(8,128)(2,1)}, u32[]{:S(2)}) copy-start(bf16[1,512,2048]{2,1,0:T(8,128)(2,1)} %param.7) | copy-start | bytes 6291460
Sparse Core Ops, SparseCore 0:
  27.2 75.9 all-gather.4
  105.5 71.8 all-gather.6
  265.6 139.5 reduce-scatter.3
  408.2 49.8 all-reduce.1
where the time goes:
time: 474 us; the launch traced here: 470 us
  waiting for transfers between devices  257 us (54%)
  other arithmetic  83.5 us (18%)
  matrix products  64.4 us (14%)
  local copies, waits for them, and re-layouts  49.7 us (10%)
  between operations  14 us (3%)
    unnamed x5, waiting for transfers between devices  134 us
    all_gather x2, waiting for transfers between devices, entering(): everything = lax.all_gather(value, axis)  89.2 us
    select_n x64, other arithmetic, step(): return jnp.where(reached, new, before)  78.8 us
    unnamed x46, local copies, waits for them, and re-layouts  42.4 us
    psum x1, waiting for transfers between devices, body(): summed = lax.psum(partial_rows, 'batch')  33.8 us
    dot_general x1, matrix products, body(): lax.dot_general(local_x, qkv_grad, (((0,), (0,)), ((), ())), preferred_el...  15.1 us
    dot_general x1, matrix products, body(): lax.dot_general(qkv_grad, w_qkv, (((1,), (1,)), ((), ())), preferred_elem...  11.7 us
    dot_general x1, matrix products, body(): jnp.dot(local_x, w_qkv, preferred_element_type=jnp.float32)  9.63 us
  transfers between devices with their start and end apart: 4, of which 4 were waited for; matrix products, arithmetic and copies ran while one was open for 17% of the time, Pallas kernels for 0%

commit v1 on v0

v1 whole, which is shorter than its diff:
```python
import functools

import jax
import jax.numpy as jnp
from jax import lax
from jax.experimental import pallas as pl
from jax.experimental.pallas import tpu as pltpu
from jax.sharding import PartitionSpec as P

HEADS = 8
DH = 128
BLK = 512
D = 2048
HALF = 512
NEAR = 4
F32 = jnp.float32
BF16 = jnp.bfloat16
AXES = ("seq", "batch")
VMEM = 40 * 1024 * 1024


def flat(x, y, c, z):
    return ((x * 4 + y) * 2 + c) * 4 + z


def every():
    for x in range(4):
        for y in range(4):
            for c in range(2):
                for z in range(4):
                    yield x, y, c, z


def shift_pairs(axis, d):
    pairs = []
    for x, y, c, z in every():
        to = dict(x=x, y=y, z=z)
        to[axis] = (to[axis] + d) % 4
        pairs.append((flat(x, y, c, z), flat(to["x"], to["y"], c, to["z"])))
    return pairs


def core_pairs():
    return [(flat(x, y, c, z), flat(x, y, 1 - c, z)) for x, y, c, z in every()]


def partner(v, kind):
    return jnp.where(kind == 0, v ^ 1, 3 - v)


def halving_pairs(axis, step):
    pairs = []
    for x, y, c, z in every():
        to = dict(x=x, y=y, z=z)
        v = to[axis]
        to[axis] = v ^ 1 if (c + step) % 2 == 0 else 3 - v
        pairs.append((flat(x, y, c, z), flat(to["x"], to["y"], c, to["z"])))
    return pairs


def permute(value, pairs):
    return lax.ppermute(value, AXES, pairs)


def params():
    return pltpu.CompilerParams(vmem_limit_bytes=VMEM)


def cost(flops, moved):
    return pl.CostEstimate(flops=flops, bytes_accessed=moved, transcendentals=0)


def dot(a, b, contract_a, contract_b):
    return lax.dot_general(
        a, b, (((contract_a,), (contract_b,)), ((), ())), preferred_element_type=F32
    )


def project_kernel(core, x_ref, w_ref, o_ref):
    del core
    o_ref[...] = dot(x_ref[...], w_ref[...], 1, 0).astype(BF16)


def project_wide_kernel(core, x_ref, w_ref, o_ref, low_ref):
    del core

    @pl.when(pl.program_id(0) == 0)
    def _():
        low_ref[...] = x_ref[...].astype(BF16)

    o_ref[...] = dot(low_ref[...], w_ref[...], 1, 0).astype(BF16)


def project(x, w, core):
    wide = x.dtype == F32
    cols = 256
    per = HALF // cols
    out_shape = [jax.ShapeDtypeStruct((BLK, 3 * HALF), BF16)]
    out_specs = [pl.BlockSpec((BLK, cols), lambda j, c: (0, j))]
    if wide:
        out_shape.append(jax.ShapeDtypeStruct((BLK, D), BF16))
        out_specs.append(pl.BlockSpec((BLK, D), lambda j, c: (0, 0)))
    return pl.pallas_call(
        project_wide_kernel if wide else project_kernel,
        out_shape=out_shape,
        grid_spec=pltpu.PrefetchScalarGridSpec(
            num_scalar_prefetch=1,
            grid=(3 * per,),
            in_specs=[
                pl.BlockSpec((BLK, D), lambda j, c: (0, 0)),
                pl.BlockSpec((D, cols), lambda j, c: (0, (j // per) * 2 * per + c[0] * per + j % per)),
            ],
            out_specs=out_specs,
        ),
        compiler_params=params(),
        cost_estimate=cost(2 * BLK * D * 3 * HALF, 12 << 20),
        name="project",
    )(core, x, w)


def state_kernel(q_ref, k_ref, v_ref, g_ref, st_ref, low_ref):
    low = g_ref[...].astype(BF16)
    low_ref[...] = low
    st_ref[0, 0] = dot(k_ref[...], v_ref[...], 0, 0)
    st_ref[0, 1] = dot(q_ref[...], low, 0, 0)


def head_spec(kind):
    return pl.BlockSpec((BLK, DH), lambda h: (0, kind * NEAR + h))


def states(proj, grad):
    return pl.pallas_call(
        state_kernel,
        out_shape=[
            jax.ShapeDtypeStruct((NEAR, 2, DH, DH), F32),
            jax.ShapeDtypeStruct((BLK, HALF), BF16),
        ],
        grid=(NEAR,),
        in_specs=[head_spec(0), head_spec(1), head_spec(2), head_spec(0)],
        out_specs=[pl.BlockSpec((1, 2, DH, DH), lambda h: (h, 0, 0, 0)), head_spec(0)],
        compiler_params=params(),
        cost_estimate=cost(4 * BLK * DH * HALF, 4 << 20),
        name="states",
    )(proj, proj, proj, grad)


def intra_kernel(q_ref, k_ref, v_ref, g_ref, att_ref, dq_ref, dk_ref, dv_ref):
    q, k, v, g = q_ref[...], k_ref[...], v_ref[...], g_ref[...]
    rows = lax.broadcasted_iota(jnp.int32, (BLK, BLK), 0)
    cols = lax.broadcasted_iota(jnp.int32, (BLK, BLK), 1)
    causal = rows >= cols
    scores = jnp.where(causal, dot(q, k, 1, 1), 0.0).astype(BF16)
    att_ref[...] = dot(scores, v, 1, 0)
    dv_ref[...] = dot(scores, g, 0, 0)
    grad_scores = jnp.where(causal, dot(g, v, 1, 1), 0.0).astype(BF16)
    dq_ref[...] = dot(grad_scores, k, 1, 0)
    dk_ref[...] = dot(grad_scores, q, 0, 0)


def intra(proj, low):
    return pl.pallas_call(
        intra_kernel,
        out_shape=[jax.ShapeDtypeStruct((BLK, HALF), F32)] * 4,
        grid=(NEAR,),
        in_specs=[head_spec(0), head_spec(1), head_spec(2), head_spec(0)],
        out_specs=[head_spec(0)] * 4,
        compiler_params=params(),
        cost_estimate=cost(12 * BLK * BLK * HALF, 6 << 20),
        name="intra",
    )(proj, proj, proj, low)


def inter_kernel(
    where, q_ref, k_ref, v_ref, g_ref, att_ref, dq_ref, dk_ref, dv_ref, st_ref,
    oatt_ref, odq_ref, odk_ref, odv_ref,
):
    kv = st_ref[0, 0].astype(BF16)
    gr = st_ref[0, 1].astype(BF16)
    position = where[1] + lax.broadcasted_iota(jnp.int32, (BLK, DH), 0)
    scale = DH ** (-0.5) / jnp.sqrt(position.astype(F32) + 1.0)
    g = g_ref[...]
    att = att_ref[...] + dot(q_ref[...], kv, 1, 0)
    oatt_ref[...] = (att * scale).astype(BF16) if oatt_ref.dtype == BF16 else att
    odq_ref[...] = (dq_ref[...] + dot(g, kv, 1, 1)).astype(BF16)
    odk_ref[...] = (dk_ref[...] + dot(v_ref[...], gr, 1, 1)).astype(BF16)
    odv_ref[...] = (dv_ref[...] + dot(k_ref[...], gr, 1, 0)).astype(BF16)


def inter(proj, low, parts, state, where, out_type):
    def at(kind):
        return pl.BlockSpec((BLK, DH), lambda j, w: (0, kind * NEAR + (w[0] - j + 4) % 4))

    return pl.pallas_call(
        inter_kernel,
        out_shape=[jax.ShapeDtypeStruct((BLK, HALF), out_type)]
        + [jax.ShapeDtypeStruct((BLK, HALF), BF16)] * 3,
        grid_spec=pltpu.PrefetchScalarGridSpec(
            num_scalar_prefetch=1,
            grid=(NEAR,),
            in_specs=[at(0), at(1), at(2), at(0)]
            + [at(0)] * 4
            + [pl.BlockSpec((1, 2, DH, DH), lambda j, w: (j, 0, 0, 0))],
            out_specs=[at(0)] * 4,
        ),
        compiler_params=params(),
        cost_estimate=cost(8 * BLK * DH * HALF, 10 << 20),
        name="inter",
    )(where, proj, proj, proj, low, *parts, state)


def turn_kernel(x_ref, o_ref):
    o_ref[...] = x_ref[...].T


def turned(value):
    return pl.pallas_call(
        turn_kernel,
        out_shape=jax.ShapeDtypeStruct((D, BLK), BF16),
        grid=(4,),
        in_specs=[pl.BlockSpec((BLK, 512), lambda j: (0, j))],
        out_specs=pl.BlockSpec((512, BLK), lambda j: (j, 0)),
        compiler_params=params(),
        cost_estimate=cost(0, 4 << 20),
        name="turned",
    )(value)


def rows_kernel(pick, xo_ref, xp_ref, do_ref, dp_ref, o_ref):
    del pick
    for y in range(4):
        at = pl.ds(y * 128, 128)
        total = dot(xo_ref[at, :], do_ref[...], 1, 0) + dot(xp_ref[at, :], dp_ref[...], 1, 0)
        for z in range(4):
            o_ref[0, y, z] = total[:, z * 128 : (z + 1) * 128]


def partial_x(xo, xp, do, dp, pick):
    left = pl.BlockSpec((512, BLK), lambda g, p: (p[g], 0))
    right = pl.BlockSpec((BLK, HALF), lambda g, p: (0, 0))
    return pl.pallas_call(
        rows_kernel,
        out_shape=jax.ShapeDtypeStruct((2, 4, 4, 128, 128), F32),
        grid_spec=pltpu.PrefetchScalarGridSpec(
            num_scalar_prefetch=1,
            grid=(2,),
            in_specs=[left, left, right, right],
            out_specs=pl.BlockSpec((1, 4, 4, 128, 128), lambda g, p: (g, 0, 0, 0, 0)),
        ),
        compiler_params=params(),
        cost_estimate=cost(2 * 1024 * 1024 * 512, 6 << 20),
        name="partial_x",
    )(pick, xo, xp, do, dp)


def short_kernel(pick, xo_ref, xp_ref, do_ref, dp_ref, o_ref):
    del pick
    total = dot(xo_ref[...], do_ref[...], 1, 0) + dot(xp_ref[...], dp_ref[...], 1, 0)
    for z in range(4):
        o_ref[0, z, 0] = total[:, z * 128 : (z + 1) * 128]


def partial_y(xo, xp, do, dp, pick):
    left = pl.BlockSpec((128, BLK), lambda g, x, p: (x * 4 + p[g], 0))
    right = pl.BlockSpec((BLK, HALF), lambda g, x, p: (0, 0))
    return pl.pallas_call(
        short_kernel,
        out_shape=jax.ShapeDtypeStruct((2, 4, 4, 128, 128), F32),
        grid_spec=pltpu.PrefetchScalarGridSpec(
            num_scalar_prefetch=1,
            grid=(2, 4),
            in_specs=[left, left, right, right],
            out_specs=pl.BlockSpec((1, 4, 1, 128, 128), lambda g, x, p: (g, 0, x, 0, 0)),
        ),
        compiler_params=params(),
        cost_estimate=cost(2 * 1024 * 1024 * 512, 6 << 20),
        name="partial_y",
    )(pick, xo, xp, do, dp)


def heads_kernel(pick, xo_ref, xp_ref, doa_ref, dob_ref, dpa_ref, dpb_ref, o_ref):
    del pick
    own = jnp.concatenate([doa_ref[...], dob_ref[...]], 1)
    other = jnp.concatenate([dpa_ref[...], dpb_ref[...]], 1)
    total = dot(xo_ref[...], own, 1, 0) + dot(xp_ref[...], other, 1, 0)
    for g in range(2):
        for y in range(4):
            o_ref[g, 0, y] = total[y * 128 : (y + 1) * 128, g * 128 : (g + 1) * 128]


def partial_z(xo, xp, do, dp, pick):
    left = pl.BlockSpec((512, BLK), lambda x, p: (x, 0))
    first = pl.BlockSpec((BLK, DH), lambda x, p: (0, p[0]))
    second = pl.BlockSpec((BLK, DH), lambda x, p: (0, p[1]))
    return pl.pallas_call(
        heads_kernel,
        out_shape=jax.ShapeDtypeStruct((2, 4, 4, 128, 128), F32),
        grid_spec=pltpu.PrefetchScalarGridSpec(
            num_scalar_prefetch=1,
            grid=(4,),
            in_specs=[left, left, first, second, first, second],
            out_specs=pl.BlockSpec((2, 1, 4, 128, 128), lambda x, p: (0, x, 0, 0, 0)),
        ),
        compiler_params=params(),
        cost_estimate=cost(2 * 1024 * 1024 * 512, 6 << 20),
        name="partial_z",
    )(pick, xo, xp, do, do, dp, dp)


def tokens_back_kernel(core, dq_ref, dk_ref, dv_ref, back_ref, w_ref, o_ref, full_ref):
    for c in range(2):

        @pl.when(jnp.logical_and(pl.program_id(0) == 0, core[0] == c))
        def _():
            for kind, own in enumerate((dq_ref, dk_ref, dv_ref)):
                full_ref[:, pl.ds((2 * kind + c) * HALF, HALF)] = own[...]
                full_ref[:, pl.ds((2 * kind + 1 - c) * HALF, HALF)] = back_ref[kind].astype(BF16)

    o_ref[...] = dot(full_ref[...], w_ref[...], 1, 1).astype(BF16)


def tokens_back(dq, dk, dv, back, w, core):
    cols = 256
    own = pl.BlockSpec((BLK, HALF), lambda j, c: (0, 0))
    return pl.pallas_call(
        tokens_back_kernel,
        out_shape=jax.ShapeDtypeStruct((BLK, D), BF16),
        grid_spec=pltpu.PrefetchScalarGridSpec(
            num_scalar_prefetch=1,
            grid=(D // cols,),
            in_specs=[
                own,
                own,
                own,
                pl.BlockSpec((3, BLK, HALF), lambda j, c: (0, 0, 0)),
                pl.BlockSpec((cols, 3072), lambda j, c: (j, 0)),
            ],
            out_specs=pl.BlockSpec((BLK, cols), lambda j, c: (0, j)),
            scratch_shapes=[pltpu.VMEM((BLK, 3072), BF16)],
        ),
        compiler_params=params(),
        cost_estimate=cost(2 * BLK * D * 3072, 20 << 20),
        name="tokens_back",
    )(core, dq, dk, dv, back, w)


def at(value, i):
    return lax.dynamic_index_in_dim(value, i, 0, keepdims=False)


def body(tokens, w_qkv, cotangent):
    s = lax.axis_index("seq")
    z = lax.axis_index("batch")
    c = s % 2
    chip = s // 2
    x = chip // 4
    y = chip % 4
    core = c.reshape(1)
    own_x = tokens[0]
    other_wide = permute(own_x.astype(F32), core_pairs())
    position = s * BLK + jnp.arange(BLK, dtype=jnp.int32)
    pos_scale = DH ** (-0.5) / jnp.sqrt(position.astype(F32) + 1.0)
    scaled = (cotangent[0].astype(F32) * pos_scale[:, None]).astype(BF16)
    own_g = lax.dynamic_slice_in_dim(scaled, c * HALF, HALF, 1)
    sent_g = lax.dynamic_slice_in_dim(scaled, (1 - c) * HALF, HALF, 1).astype(F32)
    other_g_wide = permute(sent_g, core_pairs())
    (own_p,) = project(own_x, w_qkv, core)
    own_st, own_low = states(own_p, own_g)
    other_p, other_x = project(other_wide, w_qkv, core)
    other_st, other_low = states(other_p, other_g_wide)
    chip_st = own_st + other_st
    got = [at(chip_st, y)]
    for d in range(1, 4):
        got.append(permute(at(chip_st, (y + d) % 4), shift_pairs("y", d)))
    row_kv = got[0][0] + got[1][0] + got[2][0] + got[3][0]
    row_gr = got[0][1] + got[1][1] + got[2][1] + got[3][1]
    enter_kv = jnp.zeros_like(row_kv)
    enter_gr = jnp.zeros_like(row_gr)
    for d in range(1, 4):
        came = permute(jnp.where(x + d < 4, row_kv, row_gr), shift_pairs("x", d))
        earlier = x - d >= 0
        enter_kv = enter_kv + jnp.where(earlier, came, 0.0)
        enter_gr = enter_gr + jnp.where(earlier, 0.0, came)
    back = []
    for e in range(4):
        there = (y + e) % 4
        kv, gr = enter_kv, enter_gr
        for d in range(4):
            here = (y - d + 4) % 4
            kv = kv + jnp.where(here < there, got[d][0], 0.0)
            gr = gr + jnp.where(here > there, got[d][1], 0.0)
        back.append(jnp.stack([kv, gr]))
    mine = [back[0]]
    for e in range(1, 4):
        mine.append(permute(back[e], shift_pairs("y", e)))
    state_in = jnp.stack(mine)
    order = (y - jnp.arange(4) + 4) % 4
    own_rolled = jnp.stack([at(own_st, order[j]) for j in range(4)])
    other_rolled = jnp.stack([at(other_st, order[j]) for j in range(4)])
    cf = c.astype(F32)
    pick_kv = jnp.stack([cf, 1.0 - cf]).reshape(1, 2, 1, 1)
    own_state = state_in + pick_kv * other_rolled
    other_state = state_in + (1.0 - pick_kv) * own_rolled
    own_parts = intra(own_p, own_low)
    other_parts = intra(other_p, other_low)
    xo = turned(own_x)
    xp = turned(other_x)
    own_att, own_dq, own_dk, own_dv = inter(
        own_p, own_low, own_parts, own_state, jnp.stack([y, s * BLK]), BF16
    )
    other_att, other_dq, other_dk, other_dv = inter(
        other_p, other_low, other_parts, other_state, jnp.stack([y, (s ^ 1) * BLK]), F32
    )
    place = dict(x=x, y=y, z=z)

    def picks(axis):
        v = place[axis]
        w1, w2 = partner(v, c), partner(v, 1 - c)
        return jnp.stack([w1, partner(w1, 1 - c)]), jnp.stack([v, w2])

    thirds = [
        ("xyz", partial_x, own_dq, other_dq),
        ("yzx", partial_y, own_dk, other_dk),
        ("zxy", partial_z, own_dv, other_dv),
    ]
    held = []
    for order_, make, do, dp in thirds:
        send_pick, keep_pick = picks(order_[0])
        sent = make(xo, xp, do, dp, send_pick)
        came = permute(sent, halving_pairs(order_[0], 0))
        kept = make(xo, xp, do, dp, keep_pick)
        held.append((kept, came))
    held = [
        kept[0] + came[0] + permute(kept[1] + came[1], halving_pairs(order_[0], 1))
        for (kept, came), (order_, *_) in zip(held, thirds)
    ]
    for step in (1, 2):
        after = []
        for value, (order_, *_) in zip(held, thirds):
            axis = order_[step]
            send_pick, keep_pick = picks(axis)
            sent = jnp.stack([at(value, send_pick[0]), at(value, send_pick[1])])
            came = permute(sent, halving_pairs(axis, 0))
            first = at(value, keep_pick[0]) + came[0]
            second = at(value, keep_pick[1]) + came[1]
            after.append(first + permute(second, halving_pairs(axis, 1)))
        held = after
    grad_scale = 1.0 / jnp.sqrt(F32(65536.0))
    mine_w = jnp.stack(held) * grad_scale
    mine_w = mine_w.reshape(3, 2, 64, 128)
    to_other = lax.dynamic_index_in_dim(mine_w, 1 - c, 1, keepdims=False)
    own_w = lax.dynamic_index_in_dim(mine_w, c, 1, keepdims=False)
    from_other = permute(to_other, core_pairs())
    pair = jnp.stack([jnp.where(c == 0, own_w, from_other), jnp.where(c == 0, from_other, own_w)], 1)
    all_z = [pair]
    for d in range(1, 4):
        all_z.append(permute(pair, shift_pairs("z", d)))
    stacked = jnp.stack(all_z)
    ordered = jnp.stack([at(stacked, (z - h + 4) % 4) for h in range(4)])
    weight_grad = ordered.transpose(3, 1, 2, 0, 4).reshape(64, 3072)
    att_back = permute(other_att, core_pairs())
    own_wide = own_att.astype(F32)
    att_back = att_back * pos_scale[:, None]
    attended = jnp.concatenate(
        [jnp.where(c == 0, own_wide, att_back), jnp.where(c == 0, att_back, own_wide)], 1
    ).astype(BF16)
    back_d = permute(
        jnp.stack([other_dq.astype(F32), other_dk.astype(F32), other_dv.astype(F32)]), core_pairs()
    )
    token_grad = tokens_back(own_dq, own_dk, own_dv, back_d, w_qkv, core)
    return attended[None], token_grad[None], weight_grad


def solution(mesh):
    return jax.shard_map(
        body,
        mesh=mesh,
        in_specs=(P("batch", "seq", None), P(), P("batch", "seq", None)),
        out_specs=(P("batch", "seq", None), P("batch", "seq", None), P("seq", None)),
        check_vma=False,
    )
```

time: 474 us -> 214 us (0.45)
  waiting for transfers between devices: 257 us -> 28.2 us
  Pallas kernels: 0 us -> 71.7 us
  matrix products: 64.4 us -> 0 us
  other arithmetic: 83.5 us -> 20.2 us
  starting transfers between devices: 0.16 us -> 60.8 us
  local copies, waits for them, and re-layouts: 49.7 us -> 22.8 us
  between operations: 14 us -> 9.26 us
    unnamed x5 -> x0, waiting for transfers between devices: 134 us -> none
    all_gather x2 -> x0, waiting for transfers between devices: 89.2 us -> none  [entering(): everything = lax.all_gather(value, axis)]
    select_n x64 -> x3, other arithmetic: 78.8 us -> 0.95 us  [the longest x2 0.94 us: body(): came = permute(jnp.where(x + d < 4, row_kv, row_gr), shift_pairs('x', d))]
    pallas_call x0 -> x17, Pallas kernels: none -> 71.7 us  [the longest x2 15.1 us: project(): pl.pallas_call(project_wide_kernel if wide else project_kernel, out_shape...]
    dot_general x15 -> x0, matrix products: 64.4 us -> none  [the longest x1 15.1 us: body(): lax.dot_general(local_x, qkv_grad, (((0,), (0,)), ((), ())), preferred_el...]
    ppermute x0 -> x35, starting transfers between devices: none -> 60.8 us  [permute(): return lax.ppermute(value, AXES, pairs)]
    psum x1 -> x0, waiting for transfers between devices: 33.8 us -> none  [body(): summed = lax.psum(partial_rows, 'batch')]
    ppermute x0 -> x35, waiting for transfers between devices: none -> 28.2 us  [permute(): return lax.ppermute(value, AXES, pairs)]
  transfers between devices with their start and end apart: 4 -> 35, of which waited for: 4 -> 10; matrix products, arithmetic and copies ran while one was open for 17% -> 7% of each run, Pallas kernels for 0% -> 27%
where the time goes in v1:
time: 214 us; the launch traced here: 213 us
  Pallas kernels  71.7 us (34%)
  starting transfers between devices  60.8 us (28%)
  waiting for transfers between devices  28.2 us (13%)
  local copies, waits for them, and re-layouts  22.8 us (11%)
  other arithmetic  20.2 us (9%)
  between operations  9.26 us (4%)
    ppermute x35, starting transfers between devices, permute(): return lax.ppermute(value, AXES, pairs)  60.8 us
    ppermute x35, waiting for transfers between devices, permute(): return lax.ppermute(value, AXES, pairs)  28.2 us
    unnamed x92, local copies, waits for them, and re-layouts  19.3 us
    pallas_call x2, Pallas kernels, project(): pl.pallas_call(project_wide_kernel if wide else project_kernel, out_shape...  15.1 us
    pallas_call x1, Pallas kernels, tokens_back(): pl.pallas_call(tokens_back_kernel, out_shape=jax.ShapeDtypeStruct((BLK, D...  12.3 us
    pallas_call x2, Pallas kernels, intra(): pl.pallas_call(intra_kernel, out_shape=[jax.ShapeDtypeStruct((BLK, HALF),...  10.4 us
    pallas_call x2, Pallas kernels, partial_y(): pl.pallas_call(short_kernel, out_shape=jax.ShapeDtypeStruct((2, 4, 4, 128...  8.21 us
    pallas_call x2, Pallas kernels, inter(): pl.pallas_call(inter_kernel, out_shape=[jax.ShapeDtypeStruct((BLK, HALF),...  7.52 us
  transfers between devices with their start and end apart: 35, of which 10 were waited for; matrix products, arithmetic and copies ran while one was open for 7% of the time, Pallas kernels for 27%

profile of v1, /device:TPU:1, one launch (start us, length us, event | category | flops | bytes accessed | tf_op | source)
XLA Modules:
  0.0 212.9 jit_solution(18116450999105738378)
XLA Ops:
  0.6 4.2 %bitcast_convert_fusion = f32[512,2048]{1,0:T(8,128)} fusion(bf16[1,512,2048]{2,1,0:T(8,128)(2,1)} %param.3), kind=kLoop, calls=%fused_computation.146 | loop fusion | flops 1048576 | bytes 6291456 | tf_op jit(solution)/shard_map/convert_element_type | solution.py:360
  8.3 6.8 %project.2.q_ref.k_ref.v_ref = bf16[512,1536]{1,0:T(8,128)(2,1)S(1)} custom-call(s32[1]{0:T(128)} %bitcast.2.core, bf16[512,2048]{1,0:T(8,128)(2,1)S(1)} %bitcast.236, bf16[2048,3072]{1,0:T(8,128)(2,1)} %w_ref.5), custom_call_target="tpu_custom_call" | custom-call | flops 3221225472 | bytes 12582912 | tf_op jit(solution)/shard_map/project/pallas_call | solution.py:103
  18.2 5.2 %intra.2 = (f32[512,512]{1,0:T(8,128)S(1)}, f32[512,512]{1,0:T(8,128)S(1)}, f32[512,512]{1,0:T(8,128)S(1)}, f32[512,512]{1,0:T(8,128)S(1)}) custom-call(bf16[512,1536]{1,0:T(8,128)(2,1)S(1)} %project.2.q_ref.k_ref.v_ref, bf16[512,1536]{1,0:T(8,128)(2,1)S(1)} %project.2.q_ref.k_ref.v_ref, bf16[512,1536]{1,0:T(8,128)(2,1)S(1)} %project.2.q_ref.k_ref.v_ref, ...), custom_call_target="tpu_custom_call" | custom-call | flops 1610612736 | bytes 6291456 | tf_op jit(solution)/shard_map/intra/pallas_call | solution.py:162
  27.4 8.3 %project.3 = (bf16[512,1536]{1,0:T(8,128)(2,1)S(1)}, bf16[512,2048]{1,0:T(8,128)(2,1)S(1)}) custom-call(s32[1]{0:T(128)} %bitcast.2.core, f32[512,2048]{1,0:T(8,128)} %collective-permute-done.x_ref, bf16[2048,3072]{1,0:T(8,128)(2,1)} %w_ref.5), custom_call_target="tpu_custom_call" | custom-call | flops 3221225472 | bytes 12582912 | tf_op jit(solution)/shard_map/project/pallas_call | solution.py:103
  35.7 3.3 %states.3 = (f32[4,2,128,128]{3,2,1,0:T(8,128)S(1)}, bf16[512,512]{1,0:T(8,128)(2,1)S(1)}) custom-call(bf16[512,1536]{1,0:T(8,128)(2,1)S(1)} %get-tuple-element.31.q_ref.k_ref.v_ref, bf16[512,1536]{1,0:T(8,128)(2,1)S(1)} %get-tuple-element.31.q_ref.k_ref.v_ref, bf16[512,1536]{1,0:T(8,128)(2,1)S(1)} %get-tuple-element.31.q_ref.k_ref.v_ref, ...), custom_call_target="tpu_custom_call" | custom-call | flops 134217728 | bytes 4194304 | tf_op jit(solution)/shard_map/states/pallas_call | solution.py:133
  42.2 2.6 %collective-permute-start.3 = (f32[2,128,128]{2,1,0:T(8,128)}, f32[2,128,128]{2,1,0:T(8,128)S(1)}, u32[]{:S(2)}, u32[]{:S(2)}) collective-permute-start(f32[2,128,128]{2,1,0:T(8,128)} %get-tuple-element.83), channel_id=1, source_target_pairs={{0,16},{1,17},{2,18},{3,19},{4,20},{5,21},{6,22},{7,23},{8,24},{9,... | collective-permute-start | bytes 393224 | tf_op jit(solution)/shard_map/ppermute | solution.py:62
  56.9 2.8 %collective-permute-start.6 = (f32[128,128]{1,0:T(8,128)S(1)}, f32[128,128]{1,0:T(8,128)S(1)}, u32[]{:S(2)}, u32[]{:S(2)}) collective-permute-start(f32[128,128]{1,0:T(8,128)S(1)} %get-tuple-element.99), channel_id=1, source_target_pairs={{0,64},{1,65},{2,66},{3,67},{4,68},{5,69},{6,70},{7,71},{8,72},{9,... | collective-permute-start | bytes 196616 | tf_op jit(solution)/shard_map/ppermute | solution.py:62
  63.7 5.2 %intra.3 = (f32[512,512]{1,0:T(8,128)S(1)}, f32[512,512]{1,0:T(8,128)S(1)}, f32[512,512]{1,0:T(8,128)S(1)}, f32[512,512]{1,0:T(8,128)S(1)}) custom-call(bf16[512,1536]{1,0:T(8,128)(2,1)S(1)} %copy-done.7, bf16[512,1536]{1,0:T(8,128)(2,1)S(1)} %copy-done.7, bf16[512,1536]{1,0:T(8,128)(2,1)S(1)} %copy-done.7, bf16[512,512]{1,0:T(8,128)(2,1)S(1)} %copy-done.37), custom_call_target="tpu_custom_call" | custom-call | flops 1610612736 | bytes 6291456 | tf_op jit(solution)/shard_map/intra/pallas_call | solution.py:162
  77.2 3.8 %inter.2 = (bf16[512,512]{1,0:T(8,128)(2,1)S(1)}, bf16[512,512]{1,0:T(8,128)(2,1)S(1)}, bf16[512,512]{1,0:T(8,128)(2,1)S(1)}, bf16[512,512]{1,0:T(8,128)(2,1)S(1)}) custom-call(s32[2]{0:T(128)S(1)} %pad_add_fusion.where, bf16[512,1536]{1,0:T(8,128)(2,1)S(1)} %copy-done.5, bf16[512,1536]{1,0:T(8,128)(2,1)S(1)} %copy-done.5, bf16[512,1536]{1,0:T(8,128)(2,1)S(1)} %copy-done.5, ...), custom_call_target="tpu_custom_call" | custom-call | flops 268435456 | bytes 10485760 | tf_op jit(solution)/shard_map/inter/pallas_call | solution.py:194
  81.0 3.8 %inter.3 = (f32[512,512]{1,0:T(8,128)S(1)}, bf16[512,512]{1,0:T(8,128)(2,1)S(1)}, bf16[512,512]{1,0:T(8,128)(2,1)S(1)}, bf16[512,512]{1,0:T(8,128)(2,1)S(1)}) custom-call(s32[2]{0:T(128)S(1)} %pad_add_fusion.1.where, bf16[512,1536]{1,0:T(8,128)(2,1)S(1)} %copy-done.8, bf16[512,1536]{1,0:T(8,128)(2,1)S(1)} %copy-done.8, bf16[512,1536]{1,0:T(8,128)(2,1)S(1)} %copy-done.8, ...), custom_call_target="tpu_custom_call" | custom-call | flops 268435456 | bytes 10485760 | tf_op jit(solution)/shard_map/inter/pallas_call | solution.py:194
  84.8 3.0 %partial_x.3 = f32[2,4,4,128,128]{4,3,2,1,0:T(8,128)} custom-call(s32[2]{0:T(128)S(1)} %get-tuple-element.105.pick, bf16[2048,512]{1,0:T(8,128)(2,1)S(1)} %turned.2.xo_ref, bf16[2048,512]{1,0:T(8,128)(2,1)S(1)} %turned.3.xp_ref, bf16[512,512]{1,0:T(8,128)(2,1)S(1)} %get-tuple-element.40.dq_ref.do_ref, bf16[512,512]{1,0:T(8,128)(2,1)S(1)} %get-tuple-element.43.dp_ref), custom_call_target="tpu_custom_call" | custom-call | flops 1073741824 | bytes 6291456 | tf_op jit(solution)/shard_map/partial_x/pallas_call | solution.py:241
  87.8 2.1 collective-permute-start.13
  89.9 4.9 %partial_y.3 = f32[2,4,4,128,128]{4,3,2,1,0:T(8,128)} custom-call(s32[2]{0:T(128)S(1)} %get-tuple-element.106.pick, bf16[2048,512]{1,0:T(8,128)(2,1)S(1)} %turned.2.xo_ref, bf16[2048,512]{1,0:T(8,128)(2,1)S(1)} %turned.3.xp_ref, bf16[512,512]{1,0:T(8,128)(2,1)S(1)} %get-tuple-element.41.dk_ref.do_ref, bf16[512,512]{1,0:T(8,128)(2,1)S(1)} %get-tuple-element.44.dp_ref), custom_call_target="tpu_custom_call" | custom-call | flops 1073741824 | bytes 6291456 | tf_op jit(solution)/shard_map/partial_y/pallas_call | solution.py:266
  94.9 3.7 %collective-permute-start.19 = (f32[2,4,4,128,128]{4,3,2,1,0:T(8,128)}, f32[2,4,4,128,128]{4,3,2,1,0:T(8,128)}, u32[]{:S(2)}, u32[]{:S(2)}) collective-permute-start(f32[2,4,4,128,128]{4,3,2,1,0:T(8,128)} %partial_y.3), channel_id=1, source_target_pairs={{0,8},{1,9},{2,10},{3,11},{4,28},{5,29},{6,30},{7,31},{8,0},{9,1},... | collective-permute-start | bytes 6291464 | tf_op jit(solution)/shard_map/ppermute | solution.py:62
  100.2 3.6 %partial_z.3 = f32[2,4,4,128,128]{4,3,2,1,0:T(8,128)} custom-call(s32[2]{0:T(128)S(1)} %pad_add_fusion.7.pick, bf16[2048,512]{1,0:T(8,128)(2,1)S(1)} %turned.2.xo_ref, bf16[2048,512]{1,0:T(8,128)(2,1)S(1)} %copy-done.1, bf16[512,512]{1,0:T(8,128)(2,1)S(1)} %get-tuple-element.42.dv_ref.doa_ref.dob_ref, ...), custom_call_target="tpu_custom_call" | custom-call | flops 1073741824 | bytes 6291456 | tf_op jit(solution)/shard_map/partial_z/pallas_call | solution.py:295
  103.8 3.8 %collective-permute-start.25 = (f32[2,4,4,128,128]{4,3,2,1,0:T(8,128)}, f32[2,4,4,128,128]{4,3,2,1,0:T(8,128)}, u32[]{:S(2)}, u32[]{:S(2)}) collective-permute-start(f32[2,4,4,128,128]{4,3,2,1,0:T(8,128)} %partial_z.3), channel_id=1, source_target_pairs={{0,1},{1,0},{2,3},{3,2},{4,7},{5,6},{6,5},{7,4},{8,9},{9,8},{10,11... | collective-permute-start | bytes 6291464 | tf_op jit(solution)/shard_map/ppermute | solution.py:62
  111.4 2.0 partial_x.2
  114.8 2.4 %fusion.9 = f32[4,4,128,128]{3,2,1,0:T(8,128)} fusion(f32[2,4,4,128,128]{4,3,2,1,0:T(8,128)} %collective-permute-done.13, f32[2,4,4,128,128]{4,3,2,1,0:T(8,128)S(1)} %partial_x.2), kind=kLoop, calls=%fused_computation.18 | loop fusion | flops 262144 | bytes 3145728 | tf_op jit(solution)/shard_map/add | solution.py:434
  121.0 3.3 %partial_y.2 = f32[2,4,4,128,128]{4,3,2,1,0:T(8,128)S(1)} custom-call(s32[2]{0:T(128)S(1)} %pad_add_fusion.4.pick, bf16[2048,512]{1,0:T(8,128)(2,1)S(1)} %turned.2.xo_ref, bf16[2048,512]{1,0:T(8,128)(2,1)S(1)} %copy-done.3, bf16[512,512]{1,0:T(8,128)(2,1)S(1)} %copy-done.24, bf16[512,512]{1,0:T(8,128)(2,1)S(1)} %copy-done.17), custom_call_target="tpu_custom_call" | custom-call | flops 1073741824 | bytes 6291456 | tf_op jit(solution)/shard_map/partial_y/pallas_call | solution.py:266
  127.0 6.3 %collective-permute-start.12 = (f32[3,512,512]{2,1,0:T(8,128)S(1)}, f32[3,512,512]{2,1,0:T(8,128)S(1)}, u32[]{:S(2)}, u32[]{:S(2)}) collective-permute-start(f32[3,512,512]{2,1,0:T(8,128)S(1)} %maximum_convert_fusion), channel_id=1, source_target_pairs={{0,4},{1,5},{2,6},{3,7},{4,0},{5,1},{6,2},{7,3},{8,12},{9,13},{10,... | collective-permute-start | bytes 9437192 | tf_op jit(solution)/shard_map/ppermute | solution.py:62
  134.2 2.6 %partial_z.2 = f32[2,4,4,128,128]{4,3,2,1,0:T(8,128)S(1)} custom-call(s32[2]{0:T(128)S(1)} %pad_add_fusion.6.pick, bf16[2048,512]{1,0:T(8,128)(2,1)S(1)} %turned.2.xo_ref, bf16[2048,512]{1,0:T(8,128)(2,1)S(1)} %copy-done.3, bf16[512,512]{1,0:T(8,128)(2,1)S(1)} %get-tuple-element.42.dv_ref.doa_ref.dob_ref, ...), custom_call_target="tpu_custom_call" | custom-call | flops 1073741824 | bytes 6291456 | tf_op jit(solution)/shard_map/partial_z/pallas_call | solution.py:295
  143.8 2.5 %collective-permute-start.21 = (f32[2,4,128,128]{3,2,1,0:T(8,128)S(1)}, f32[2,4,128,128]{3,2,1,0:T(8,128)S(1)}, u32[]{:S(2)}, u32[]{:S(2)}) collective-permute-start(f32[2,4,128,128]{3,2,1,0:T(8,128)S(1)} %pad_maximum_fusion.4), channel_id=1, source_target_pairs={{0,1},{1,0},{2,3},{3,2},{4,7},{5,6},{6,5},{7,4},{8,9},{9,8},{10,11... | collective-permute-start | bytes 1572872 | tf_op jit(solution)/shard_map/ppermute | solution.py:62
  146.3 6.3 %collective-permute-done.26 = f32[4,4,128,128]{3,2,1,0:T(8,128)S(1)} collective-permute-done((f32[4,4,128,128]{3,2,1,0:T(8,128)S(1)}, f32[4,4,128,128]{3,2,1,0:T(8,128)S(1)}, u32[]{:S(2)}, u32[]{:S(2)}) %collective-permute-start.26) | collective-permute-done | bytes 1048608 | tf_op jit(solution)/shard_map/ppermute | solution.py:62
  155.4 3.7 %collective-permute-done.21 = f32[2,4,128,128]{3,2,1,0:T(8,128)S(1)} collective-permute-done((f32[2,4,128,128]{3,2,1,0:T(8,128)S(1)}, f32[2,4,128,128]{3,2,1,0:T(8,128)S(1)}, u32[]{:S(2)}, u32[]{:S(2)}) %collective-permute-start.21) | collective-permute-done | bytes 524320 | tf_op jit(solution)/shard_map/ppermute | solution.py:62
  159.5 3.9 %collective-permute-done.27 = f32[2,4,128,128]{3,2,1,0:T(8,128)S(1)} collective-permute-done((f32[2,4,128,128]{3,2,1,0:T(8,128)S(1)}, f32[2,4,128,128]{3,2,1,0:T(8,128)S(1)}, u32[]{:S(2)}, u32[]{:S(2)}) %collective-permute-start.27) | collective-permute-done | bytes 524320 | tf_op jit(solution)/shard_map/ppermute | solution.py:62
  163.6 3.7 %collective-permute-start.17 = (f32[2,128,128]{2,1,0:T(8,128)S(1)}, f32[2,128,128]{2,1,0:T(8,128)S(1)}, u32[]{:S(2)}, u32[]{:S(2)}) collective-permute-start(f32[2,128,128]{2,1,0:T(8,128)S(1)} %pad_maximum_fusion.10), channel_id=1, source_target_pairs={{0,1},{1,0},{2,3},{3,2},{4,7},{5,6},{6,5},{7,4},{8,9},{9,8},{10,11... | collective-permute-start | bytes 393224 | tf_op jit(solution)/shard_map/ppermute | solution.py:62
  168.1 3.7 %collective-permute-done.28 = f32[4,128,128]{2,1,0:T(8,128)S(1)} collective-permute-done((f32[4,128,128]{2,1,0:T(8,128)S(1)}, f32[4,128,128]{2,1,0:T(8,128)S(1)}, u32[]{:S(2)}, u32[]{:S(2)}) %collective-permute-start.28) | collective-permute-done | bytes 262176 | tf_op jit(solution)/shard_map/ppermute | solution.py:62
  173.8 3.2 %collective-permute-done.29 = f32[2,128,128]{2,1,0:T(8,128)S(1)} collective-permute-done((f32[2,128,128]{2,1,0:T(8,128)S(1)}, f32[2,128,128]{2,1,0:T(8,128)S(1)}, u32[]{:S(2)}, u32[]{:S(2)}) %collective-permute-start.29) | collective-permute-done | bytes 131104 | tf_op jit(solution)/shard_map/ppermute | solution.py:62
  177.4 3.3 %collective-permute-done.30 = f32[128,128]{1,0:T(8,128)S(1)} collective-permute-done((f32[128,128]{1,0:T(8,128)S(1)}, f32[128,128]{1,0:T(8,128)S(1)}, u32[]{:S(2)}, u32[]{:S(2)}) %collective-permute-start.30) | collective-permute-done | bytes 65568 | tf_op jit(solution)/shard_map/ppermute | solution.py:62
  180.8 12.5 %collective-permute-start.31 = (f32[3,64,128]{2,1,0:T(8,128)S(1)}, f32[3,64,128]{2,1,0:T(8,128)S(1)}, u32[]{:S(2)}, u32[]{:S(2)}) collective-permute-start(f32[3,64,128]{2,1,0:T(8,128)S(1)} %dynamic-slice_bitcast_fusion.3), channel_id=1, source_target_pairs={{0,4},{1,5},{2,6},{3,7},{4,0},{5,1},{6,2},{7,3},{8,12},{9,13},{10,... | collective-permute-start | bytes 294920 | tf_op jit(solution)/shard_map/ppermute | solution.py:62
  194.5 4.1 %collective-permute-start.33 = (f32[3,2,64,128]{3,2,0,1:T(8,128)S(1)}, f32[3,2,64,128]{3,2,0,1:T(8,128)S(1)}, u32[]{:S(2)}, u32[]{:S(2)}) collective-permute-start(f32[3,2,64,128]{3,2,0,1:T(8,128)S(1)} %get-tuple-element.98), channel_id=1, source_target_pairs={{0,2},{1,3},{2,0},{3,1},{4,6},{5,7},{6,4},{7,5},{8,10},{9,11},{10,... | collective-permute-start | bytes 589832 | tf_op jit(solution)/shard_map/ppermute | solution.py:62
  198.7 12.3 %tokens_back.1 = bf16[512,2048]{1,0:T(8,128)(2,1)} custom-call(s32[1]{0:T(128)} %bitcast.2.core, bf16[512,512]{1,0:T(8,128)(2,1)S(1)} %copy-done.22, bf16[512,512]{1,0:T(8,128)(2,1)S(1)} %copy-done.25, bf16[512,512]{1,0:T(8,128)(2,1)S(1)} %get-tuple-element.42.dv_ref.doa_ref.dob_ref, f32[3,512,512]{2,1,0:T(8,128)S(1)} %collective-permute-done.12.back_ref, ...), custom_call_target="tpu_custom_call" | custom-call | flops 6442450944 | bytes 20971520 | tf_op jit(solution)/shard_map/tokens_back/pallas_call | solution.py:325
  (218 shorter events, 60.8 us)
Async XLA Ops:
  4.9 22.5 %collective-permute-start = (f32[512,2048]{1,0:T(8,128)}, f32[512,2048]{1,0:T(8,128)}, u32[]{:S(2)}, u32[]{:S(2)}) collective-permute-start(f32[512,2048]{1,0:T(8,128)} %bitcast_convert_fusion), channel_id=1, source_target_pairs={{0,4},{1,5},{2,6},{3,7},{4,0},{5,1},{6,2},{7,3},{8,12},{9,13},{10,... | collective-permute-start | bytes 12582920 | tf_op jit(solution)/shard_map/ppermute | solution.py:62
  7.7 28.0 %collective-permute-start.1 = (f32[512,512]{1,0:T(8,128)}, f32[512,512]{1,0:T(8,128)}, u32[]{:S(2)}, u32[]{:S(2)}) collective-permute-start(f32[512,512]{1,0:T(8,128)} %get-tuple-element.64), channel_id=1, source_target_pairs={{0,4},{1,5},{2,6},{3,7},{4,0},{5,1},{6,2},{7,3},{8,12},{9,13},{10,... | collective-permute-start | bytes 3145736 | tf_op jit(solution)/shard_map/ppermute | solution.py:62
  40.8 15.2 %collective-permute-start.2 = (f32[2,128,128]{2,1,0:T(8,128)}, f32[2,128,128]{2,1,0:T(8,128)S(1)}, u32[]{:S(2)}, u32[]{:S(2)}) collective-permute-start(f32[2,128,128]{2,1,0:T(8,128)} %get-tuple-element.84), channel_id=1, source_target_pairs={{0,8},{1,9},{2,10},{3,11},{4,12},{5,13},{6,14},{7,15},{8,16},{9,17... | collective-permute-start | bytes 393224 | tf_op jit(solution)/shard_map/ppermute | solution.py:62
  42.2 13.8 %collective-permute-start.3 = (f32[2,128,128]{2,1,0:T(8,128)}, f32[2,128,128]{2,1,0:T(8,128)S(1)}, u32[]{:S(2)}, u32[]{:S(2)}) collective-permute-start(f32[2,128,128]{2,1,0:T(8,128)} %get-tuple-element.83), channel_id=1, source_target_pairs={{0,16},{1,17},{2,18},{3,19},{4,20},{5,21},{6,22},{7,23},{8,24},{9,... | collective-permute-start | bytes 393224 | tf_op jit(solution)/shard_map/ppermute | solution.py:62
  44.8 11.2 %collective-permute-start.4 = (f32[2,128,128]{2,1,0:T(8,128)}, f32[2,128,128]{2,1,0:T(8,128)S(1)}, u32[]{:S(2)}, u32[]{:S(2)}) collective-permute-start(f32[2,128,128]{2,1,0:T(8,128)} %get-tuple-element.82), channel_id=1, source_target_pairs={{0,24},{1,25},{2,26},{3,27},{4,28},{5,29},{6,30},{7,31},{8,0},{9,1... | collective-permute-start | bytes 393224 | tf_op jit(solution)/shard_map/ppermute | solution.py:62
  56.9 11.9 %collective-permute-start.6 = (f32[128,128]{1,0:T(8,128)S(1)}, f32[128,128]{1,0:T(8,128)S(1)}, u32[]{:S(2)}, u32[]{:S(2)}) collective-permute-start(f32[128,128]{1,0:T(8,128)S(1)} %get-tuple-element.99), channel_id=1, source_target_pairs={{0,64},{1,65},{2,66},{3,67},{4,68},{5,69},{6,70},{7,71},{8,72},{9,... | collective-permute-start | bytes 196616 | tf_op jit(solution)/shard_map/ppermute | solution.py:62
  59.7 9.1 %collective-permute-start.7 = (f32[128,128]{1,0:T(8,128)S(1)}, f32[128,128]{1,0:T(8,128)S(1)}, u32[]{:S(2)}, u32[]{:S(2)}) collective-permute-start(f32[128,128]{1,0:T(8,128)S(1)} %get-tuple-element.100), channel_id=1, source_target_pairs={{0,96},{1,97},{2,98},{3,99},{4,100},{5,101},{6,102},{7,103},{8,104... | collective-permute-start | bytes 196616 | tf_op jit(solution)/shard_map/ppermute | solution.py:62
  60.6 8.3 %collective-permute-start.5 = (f32[128,128]{1,0:T(8,128)S(1)}, f32[128,128]{1,0:T(8,128)S(1)}, u32[]{:S(2)}, u32[]{:S(2)}) collective-permute-start(f32[128,128]{1,0:T(8,128)S(1)} %get-tuple-element.53), channel_id=1, source_target_pairs={{0,32},{1,33},{2,34},{3,35},{4,36},{5,37},{6,38},{7,39},{8,40},{9,... | collective-permute-start | bytes 196616 | tf_op jit(solution)/shard_map/ppermute | solution.py:62
  69.1 5.8 %collective-permute-start.8 = (f32[2,128,128]{2,1,0:T(8,128)S(1)}, f32[2,128,128]{2,1,0:T(8,128)S(1)}, u32[]{:S(2)}, u32[]{:S(2)}) collective-permute-start(f32[2,128,128]{2,1,0:T(8,128)S(1)} %pad_maximum_fusion.7), channel_id=1, source_target_pairs={{0,8},{1,9},{2,10},{3,11},{4,12},{5,13},{6,14},{7,15},{8,16},{9,17... | collective-permute-start | bytes 393224 | tf_op jit(solution)/shard_map/ppermute | solution.py:62
  69.6 6.4 %collective-permute-start.9 = (f32[2,128,128]{2,1,0:T(8,128)S(1)}, f32[2,128,128]{2,1,0:T(8,128)S(1)}, u32[]{:S(2)}, u32[]{:S(2)}) collective-permute-start(f32[2,128,128]{2,1,0:T(8,128)S(1)} %pad_maximum_fusion.8), channel_id=1, source_target_pairs={{0,16},{1,17},{2,18},{3,19},{4,20},{5,21},{6,22},{7,23},{8,24},{9,... | collective-permute-start | bytes 393224 | tf_op jit(solution)/shard_map/ppermute | solution.py:62
  70.5 6.4 %collective-permute-start.10 = (f32[2,128,128]{2,1,0:T(8,128)S(1)}, f32[2,128,128]{2,1,0:T(8,128)S(1)}, u32[]{:S(2)}, u32[]{:S(2)}) collective-permute-start(f32[2,128,128]{2,1,0:T(8,128)S(1)} %pad_maximum_fusion.9), channel_id=1, source_target_pairs={{0,24},{1,25},{2,26},{3,27},{4,28},{5,29},{6,30},{7,31},{8,0},{9,1... | collective-permute-start | bytes 393224 | tf_op jit(solution)/shard_map/ppermute | solution.py:62
  87.8 26.4 %collective-permute-start.13 = (f32[2,4,4,128,128]{4,3,2,1,0:T(8,128)}, f32[2,4,4,128,128]{4,3,2,1,0:T(8,128)}, u32[]{:S(2)}, u32[]{:S(2)}) collective-permute-start(f32[2,4,4,128,128]{4,3,2,1,0:T(8,128)} %partial_x.3), channel_id=1, source_target_pairs={{0,32},{1,33},{2,34},{3,35},{4,100},{5,101},{6,102},{7,103},{8,40}... | collective-permute-start | bytes 6291464 | tf_op jit(solution)/shard_map/ppermute | solution.py:62
  94.9 29.5 %collective-permute-start.19 = (f32[2,4,4,128,128]{4,3,2,1,0:T(8,128)}, f32[2,4,4,128,128]{4,3,2,1,0:T(8,128)}, u32[]{:S(2)}, u32[]{:S(2)}) collective-permute-start(f32[2,4,4,128,128]{4,3,2,1,0:T(8,128)} %partial_y.3), channel_id=1, source_target_pairs={{0,8},{1,9},{2,10},{3,11},{4,28},{5,29},{6,30},{7,31},{8,0},{9,1},... | collective-permute-start | bytes 6291464 | tf_op jit(solution)/shard_map/ppermute | solution.py:62
  103.8 33.0 %collective-permute-start.25 = (f32[2,4,4,128,128]{4,3,2,1,0:T(8,128)}, f32[2,4,4,128,128]{4,3,2,1,0:T(8,128)}, u32[]{:S(2)}, u32[]{:S(2)}) collective-permute-start(f32[2,4,4,128,128]{4,3,2,1,0:T(8,128)} %partial_z.3), channel_id=1, source_target_pairs={{0,1},{1,0},{2,3},{3,2},{4,7},{5,6},{6,5},{7,4},{8,9},{9,8},{10,11... | collective-permute-start | bytes 6291464 | tf_op jit(solution)/shard_map/ppermute | solution.py:62
  117.2 22.9 %collective-permute-start.14 = (f32[4,4,128,128]{3,2,1,0:T(8,128)}, f32[4,4,128,128]{3,2,1,0:T(8,128)}, u32[]{:S(2)}, u32[]{:S(2)}) collective-permute-start(f32[4,4,128,128]{3,2,1,0:T(8,128)} %fusion.9), channel_id=1, source_target_pairs={{0,96},{1,97},{2,98},{3,99},{4,36},{5,37},{6,38},{7,39},{8,104},{9... | collective-permute-start | bytes 3145736 | tf_op jit(solution)/shard_map/ppermute | solution.py:62
  125.7 16.6 %collective-permute-start.20 = (f32[4,4,128,128]{3,2,1,0:T(8,128)S(1)}, f32[4,4,128,128]{3,2,1,0:T(8,128)S(1)}, u32[]{:S(2)}, u32[]{:S(2)}) collective-permute-start(f32[4,4,128,128]{3,2,1,0:T(8,128)S(1)} %fusion.6), channel_id=1, source_target_pairs={{0,24},{1,25},{2,26},{3,27},{4,12},{5,13},{6,14},{7,15},{8,16},{9,... | collective-permute-start | bytes 3145736 | tf_op jit(solution)/shard_map/ppermute | solution.py:62
  127.0 71.6 %collective-permute-start.12 = (f32[3,512,512]{2,1,0:T(8,128)S(1)}, f32[3,512,512]{2,1,0:T(8,128)S(1)}, u32[]{:S(2)}, u32[]{:S(2)}) collective-permute-start(f32[3,512,512]{2,1,0:T(8,128)S(1)} %maximum_convert_fusion), channel_id=1, source_target_pairs={{0,4},{1,5},{2,6},{3,7},{4,0},{5,1},{6,2},{7,3},{8,12},{9,13},{10,... | collective-permute-start | bytes 9437192 | tf_op jit(solution)/shard_map/ppermute | solution.py:62
  133.3 21.5 %collective-permute-start.11 = (f32[512,512]{1,0:T(8,128)S(1)}, f32[512,512]{1,0:T(8,128)S(1)}, u32[]{:S(2)}, u32[]{:S(2)}) collective-permute-start(f32[512,512]{1,0:T(8,128)S(1)} %copy-done.41), channel_id=1, source_target_pairs={{0,4},{1,5},{2,6},{3,7},{4,0},{5,1},{6,2},{7,3},{8,12},{9,13},{10,... | collective-permute-start | bytes 3145736 | tf_op jit(solution)/shard_map/ppermute | solution.py:62
  138.4 14.2 %collective-permute-start.26 = (f32[4,4,128,128]{3,2,1,0:T(8,128)S(1)}, f32[4,4,128,128]{3,2,1,0:T(8,128)S(1)}, u32[]{:S(2)}, u32[]{:S(2)}) collective-permute-start(f32[4,4,128,128]{3,2,1,0:T(8,128)S(1)} %fusion.3), channel_id=1, source_target_pairs={{0,3},{1,2},{2,1},{3,0},{4,5},{5,4},{6,7},{7,6},{8,11},{9,10},{10,... | collective-permute-start | bytes 3145736 | tf_op jit(solution)/shard_map/ppermute | solution.py:62
  141.9 13.4 %collective-permute-start.15 = (f32[2,4,128,128]{3,2,1,0:T(8,128)S(1)}, f32[2,4,128,128]{3,2,1,0:T(8,128)S(1)}, u32[]{:S(2)}, u32[]{:S(2)}) collective-permute-start(f32[2,4,128,128]{3,2,1,0:T(8,128)S(1)} %pad_maximum_fusion.3), channel_id=1, source_target_pairs={{0,8},{1,9},{2,10},{3,11},{4,28},{5,29},{6,30},{7,31},{8,0},{9,1},... | collective-permute-start | bytes 1572872 | tf_op jit(solution)/shard_map/ppermute | solution.py:62
  143.8 15.3 %collective-permute-start.21 = (f32[2,4,128,128]{3,2,1,0:T(8,128)S(1)}, f32[2,4,128,128]{3,2,1,0:T(8,128)S(1)}, u32[]{:S(2)}, u32[]{:S(2)}) collective-permute-start(f32[2,4,128,128]{3,2,1,0:T(8,128)S(1)} %pad_maximum_fusion.4), channel_id=1, source_target_pairs={{0,1},{1,0},{2,3},{3,2},{4,7},{5,6},{6,5},{7,4},{8,9},{9,8},{10,11... | collective-permute-start | bytes 1572872 | tf_op jit(solution)/shard_map/ppermute | solution.py:62
  154.1 9.3 %collective-permute-start.27 = (f32[2,4,128,128]{3,2,1,0:T(8,128)S(1)}, f32[2,4,128,128]{3,2,1,0:T(8,128)S(1)}, u32[]{:S(2)}, u32[]{:S(2)}) collective-permute-start(f32[2,4,128,128]{3,2,1,0:T(8,128)S(1)} %pad_maximum_fusion.5), channel_id=1, source_target_pairs={{0,32},{1,33},{2,34},{3,35},{4,100},{5,101},{6,102},{7,103},{8,40}... | collective-permute-start | bytes 1572872 | tf_op jit(solution)/shard_map/ppermute | solution.py:62
  155.3 8.2 %collective-permute-start.16 = (f32[4,128,128]{2,1,0:T(8,128)S(1)}, f32[4,128,128]{2,1,0:T(8,128)S(1)}, u32[]{:S(2)}, u32[]{:S(2)}) collective-permute-start(f32[4,128,128]{2,1,0:T(8,128)S(1)} %fusion.22), channel_id=1, source_target_pairs={{0,24},{1,25},{2,26},{3,27},{4,12},{5,13},{6,14},{7,15},{8,16},{9,... | collective-permute-start | bytes 786440 | tf_op jit(solution)/shard_map/ppermute | solution.py:62
  159.1 8.2 %collective-permute-start.22 = (f32[4,128,128]{2,1,0:T(8,128)S(1)}, f32[4,128,128]{2,1,0:T(8,128)S(1)}, u32[]{:S(2)}, u32[]{:S(2)}) collective-permute-start(f32[4,128,128]{2,1,0:T(8,128)S(1)} %fusion.19), channel_id=1, source_target_pairs={{0,3},{1,2},{2,1},{3,0},{4,5},{5,4},{6,7},{7,6},{8,11},{9,10},{10,... | collective-permute-start | bytes 786440 | tf_op jit(solution)/shard_map/ppermute | solution.py:62
  163.4 8.3 %collective-permute-start.28 = (f32[4,128,128]{2,1,0:T(8,128)S(1)}, f32[4,128,128]{2,1,0:T(8,128)S(1)}, u32[]{:S(2)}, u32[]{:S(2)}) collective-permute-start(f32[4,128,128]{2,1,0:T(8,128)S(1)} %fusion.16), channel_id=1, source_target_pairs={{0,96},{1,97},{2,98},{3,99},{4,36},{5,37},{6,38},{7,39},{8,104},{9... | collective-permute-start | bytes 786440 | tf_op jit(solution)/shard_map/ppermute | solution.py:62
  163.6 8.7 %collective-permute-start.17 = (f32[2,128,128]{2,1,0:T(8,128)S(1)}, f32[2,128,128]{2,1,0:T(8,128)S(1)}, u32[]{:S(2)}, u32[]{:S(2)}) collective-permute-start(f32[2,128,128]{2,1,0:T(8,128)S(1)} %pad_maximum_fusion.10), channel_id=1, source_target_pairs={{0,1},{1,0},{2,3},{3,2},{4,7},{5,6},{6,5},{7,4},{8,9},{9,8},{10,11... | collective-permute-start | bytes 393224 | tf_op jit(solution)/shard_map/ppermute | solution.py:62
  167.4 6.3 %collective-permute-start.23 = (f32[2,128,128]{2,1,0:T(8,128)S(1)}, f32[2,128,128]{2,1,0:T(8,128)S(1)}, u32[]{:S(2)}, u32[]{:S(2)}) collective-permute-start(f32[2,128,128]{2,1,0:T(8,128)S(1)} %pad_maximum_fusion.11), channel_id=1, source_target_pairs={{0,32},{1,33},{2,34},{3,35},{4,100},{5,101},{6,102},{7,103},{8,40}... | collective-permute-start | bytes 393224 | tf_op jit(solution)/shard_map/ppermute | solution.py:62
  171.9 5.1 %collective-permute-start.29 = (f32[2,128,128]{2,1,0:T(8,128)S(1)}, f32[2,128,128]{2,1,0:T(8,128)S(1)}, u32[]{:S(2)}, u32[]{:S(2)}) collective-permute-start(f32[2,128,128]{2,1,0:T(8,128)S(1)} %pad_maximum_fusion.12), channel_id=1, source_target_pairs={{0,8},{1,9},{2,10},{3,11},{4,28},{5,29},{6,30},{7,31},{8,0},{9,1},... | collective-permute-start | bytes 393224 | tf_op jit(solution)/shard_map/ppermute | solution.py:62
  180.8 13.6 %collective-permute-start.31 = (f32[3,64,128]{2,1,0:T(8,128)S(1)}, f32[3,64,128]{2,1,0:T(8,128)S(1)}, u32[]{:S(2)}, u32[]{:S(2)}) collective-permute-start(f32[3,64,128]{2,1,0:T(8,128)S(1)} %dynamic-slice_bitcast_fusion.3), channel_id=1, source_target_pairs={{0,4},{1,5},{2,6},{3,7},{4,0},{5,1},{6,2},{7,3},{8,12},{9,13},{10,... | collective-permute-start | bytes 294920 | tf_op jit(solution)/shard_map/ppermute | solution.py:62
  194.4 16.5 %collective-permute-start.32 = (f32[3,2,64,128]{3,2,0,1:T(8,128)S(1)}, f32[3,2,64,128]{3,2,0,1:T(8,128)S(1)}, u32[]{:S(2)}, u32[]{:S(2)}) collective-permute-start(f32[3,2,64,128]{3,2,0,1:T(8,128)S(1)} %get-tuple-element.98), channel_id=1, source_target_pairs={{0,1},{1,2},{2,3},{3,0},{4,5},{5,6},{6,7},{7,4},{8,9},{9,10},{10,1... | collective-permute-start | bytes 589832 | tf_op jit(solution)/shard_map/ppermute | solution.py:62
  194.5 16.5 %collective-permute-start.33 = (f32[3,2,64,128]{3,2,0,1:T(8,128)S(1)}, f32[3,2,64,128]{3,2,0,1:T(8,128)S(1)}, u32[]{:S(2)}, u32[]{:S(2)}) collective-permute-start(f32[3,2,64,128]{3,2,0,1:T(8,128)S(1)} %get-tuple-element.98), channel_id=1, source_target_pairs={{0,2},{1,3},{2,0},{3,1},{4,6},{5,7},{6,4},{7,5},{8,10},{9,11},{10,... | collective-permute-start | bytes 589832 | tf_op jit(solution)/shard_map/ppermute | solution.py:62
  198.6 12.3 %collective-permute-start.34 = (f32[3,2,64,128]{3,2,0,1:T(8,128)S(1)}, f32[3,2,64,128]{3,2,0,1:T(8,128)S(1)}, u32[]{:S(2)}, u32[]{:S(2)}) collective-permute-start(f32[3,2,64,128]{3,2,0,1:T(8,128)S(1)} %get-tuple-element.98), channel_id=1, source_target_pairs={{0,3},{1,0},{2,1},{3,2},{4,7},{5,4},{6,5},{7,6},{8,11},{9,8},{10,9... | collective-permute-start | bytes 589832 | tf_op jit(solution)/shard_map/ppermute | solution.py:62
  (49 other events, 204.0 us)
